TPU v7x, 32 devices: a whole 2x2x4 slice. The times are simulated.
32 devices in a mesh: row: 4 (over y, core), col: 8 (over z, x).
Axes of the slice: x: 2, y: 2, z: 4, core: 2. Of those that a mesh axis runs over, the one named last changes fastest.
Arguments:
- rhs: float32 [512, 4096], P('col', 'row'), may hold values from -6 to 6
- couple_prev: float32 [4096, 1024], P('row'), may hold values from -0.1875 to 0.1875
- diag_inverse: float32 [4096, 1024], P('row'), may hold values from -2 to 2
- coupling: bfloat16 [384, 16, 128], P(('row', 'col')), may hold values from -0.5 to 0.5
- pair_block: int32 [384], P(('row', 'col')), may hold values from 0 to 31, as said below
- pair_tile: int32 [384], P(('row', 'col')), may hold values from 0 to 2
- pair_count: int32 [32], P(('row', 'col')), may hold values from 8 to 12, as said below
- owner_slot: int32 [4, 24], P('row'), may hold values from 0 to 23, each once within a row
- schur: bfloat16 [1536, 32768], P('row', 'col'), may hold values from -6 to 6
- surface_factor: bfloat16 [512, 32768], P(None, 'col'), may hold values from -0.125 to 0.125
Outputs:
- updated: bfloat16 [1536, 32768], P('row', 'col')
Inputs may be any that keep to these rules, and one draw needn't show every extreme that they name: Among the first pair_count entries of one owner, at most 3 name blocks whose block-row group pair_block // 8 is the same; some owner has exactly 3 from one group. `pair_count`: some owner has 12 live coupling tiles.
All inputs are finite; a program needn't handle non-finite values.
Results may differ from a plain program's by a relative error of at most 0.0055.
Values may be sent and summed in bfloat16 or wider, within the bound.
A program may use at most 128 MiB of HBM per device.

v0:
```python
import functools

import jax
import jax.numpy as jnp
from jax import lax
from jax.experimental import pallas as pl
from jax.experimental.pallas import tpu as pltpu
from jax.sharding import PartitionSpec as P

CAP = 3
F32 = jnp.float32
BF16 = jnp.bfloat16
NT = (((1,), (1,)), ((), ()))


def dot(left, right):
    return jnp.dot(left, right, preferred_element_type=F32)


def halves(value):
    high = value.astype(BF16)
    return high, (value - high.astype(F32)).astype(BF16)


def kernel(
    n_rows,
    n_cols,
    rhs_hbm,
    couple_hbm,
    inverse_hbm,
    coupling_hbm,
    block_hbm,
    tile_hbm,
    count_hbm,
    slot_hbm,
    out,
    rhs,
    couple,
    inverse,
    coupling,
    block_ref,
    tile_ref,
    count_ref,
    slot_ref,
    couple_hi,
    inverse_hi,
    inverse_lo,
    chunks,
    gathered,
    dense,
    order,
    solved,
    before,
    right,
    partial,
    arrived,
    turned,
    load_sem,
    swap_send,
    swap_recv,
    share_send,
    share_recv,
    hop_sem,
    part_send,
    part_recv,
    turn_send,
    turn_recv,
):
    my_row = lax.axis_index("row")
    my_col = lax.axis_index("col")
    cols, width = rhs.shape
    held, tile, blk = coupling.shape
    per_row = width // blk
    tpr = slot_ref.shape[1]
    tpd = tpr // n_cols
    group = tpr * tile

    pairs = [
        (block_hbm, block_ref),
        (tile_hbm, tile_ref),
        (count_hbm, count_ref),
        (coupling_hbm, coupling),
        (inverse_hbm, inverse),
        (rhs_hbm, rhs),
        (couple_hbm, couple),
        (slot_hbm, slot_ref),
    ]
    loads = [
        pltpu.make_async_copy(source, target, load_sem.at[i])
        for i, (source, target) in enumerate(pairs)
    ]
    for load in loads:
        load.start()

    def row_peer(step):
        return {"row": lax.rem(my_row + step, n_rows)}

    def col_peer(step):
        return {"col": lax.rem(my_col + step, n_cols)}

    pair = 2 if n_cols % 2 == 0 else 1
    line = n_cols // pair

    def pair_up(send, recv, block):
        lane = lax.rem(my_col, pair)
        major = my_col // pair
        near, far = [], []

        def push(index, target, number):
            return pltpu.make_async_remote_copy(
                src_ref=block(index),
                dst_ref=block(index),
                send_sem=send.at[number],
                recv_sem=recv.at[number],
                device_id={"col": target},
                device_id_type=pl.DeviceIdType.MESH,
            )

        for step in range(1, line):
            near.append(push(my_col, lax.rem(major + step, line) * pair + lane, step))
        for step in range(line):
            source = lax.rem(major + line - step, line) * pair + lane
            if pair > 1:
                far.append(push(source, major * pair + 1 - lane, line + step))
        return near, far

    def forward(near, far):
        for step in range(1, line):
            near[step - 1].wait_recv()
            for copy in far[step : step + 1]:
                copy.start()

    barrier = pltpu.get_barrier_semaphore()
    for step in range(1, n_rows):
        pl.semaphore_signal(
            barrier, inc=1, device_id=row_peer(step), device_id_type=pl.DeviceIdType.MESH
        )
    for step in range(1, n_cols):
        pl.semaphore_signal(
            barrier, inc=1, device_id=col_peer(step), device_id_type=pl.DeviceIdType.MESH
        )

    for load in loads[:4]:
        load.wait()

    count = count_ref[0]
    keys, codes = [], []
    sources = []
    for k in range(held):
        block = block_ref[k]
        source = lax.div(block, per_row)
        rank = jnp.int32(0)
        for j in range(k):
            rank = rank + jnp.where(sources[j] == source, 1, 0)
        sources.append(jnp.where(k < count, source, -1))
        keys.append(jnp.where(k < count, source * CAP + rank, -1))
        codes.append(tile_ref[k] * per_row + block - source * per_row)
    lines = lax.broadcasted_iota(jnp.int32, (tile, blk), 0)
    for r in range(n_rows):
        marks = jnp.full((tile, blk), -1, jnp.int32)
        for s in range(CAP):
            place, code = jnp.int32(0), jnp.int32(-1)
            for k in range(held):
                hit = keys[k] == r * CAP + s
                place = jnp.where(hit, k, place)
                code = jnp.where(hit, codes[k], code)
            chunks[r, s * tile : (s + 1) * tile, :] = coupling[place]
            marks = jnp.where(lines == s, code, marks)
        chunks[r, CAP * tile : (CAP + 1) * tile, :] = marks.astype(F32).astype(BF16)
    gathered[my_col, my_row] = chunks[my_row]

    pl.semaphore_wait(barrier, n_rows + n_cols - 2)

    swaps = []
    for step in range(1, n_rows):
        swap = pltpu.make_async_remote_copy(
            src_ref=chunks.at[lax.rem(my_row + step, n_rows)],
            dst_ref=gathered.at[my_col, my_row],
            send_sem=swap_send.at[step],
            recv_sem=swap_recv.at[step],
            device_id=row_peer(step),
            device_id_type=pl.DeviceIdType.MESH,
        )
        swap.start()
        swaps.append(swap)

    loads[4].wait()
    loads[5].wait()
    high, low = halves(inverse[...])
    inverse_hi[...] = high
    inverse_lo[...] = low
    loads[6].wait()
    loads[7].wait()

    @pl.when(my_row > 0)
    def _():
        couple_hi[...] = couple[...].astype(BF16)

    for swap in swaps:
        swap.wait()
    near, far = pair_up(share_send, share_recv, lambda index: gathered.at[index])
    for copy in far[:1] + near:
        copy.start()

    hop = pltpu.make_async_remote_copy(
        src_ref=solved,
        dst_ref=before,
        send_sem=hop_sem.at[0],
        recv_sem=hop_sem.at[1],
        device_id=row_peer(1),
        device_id_type=pl.DeviceIdType.MESH,
    )

    def chain():
        right[...] = rhs[...]

        @pl.when(my_row > 0)
        def _():
            hop.wait_recv()
            known = before[...]
            right[...] = rhs[...] - dot(known, couple_hi[...])

        high, low = halves(right[...])
        both = dot(jnp.concatenate([high, low], axis=0), inverse_hi[...])
        solved[...] = (both[:cols] + both[cols:] + dot(high, inverse_lo[...])).astype(BF16)

    half = n_rows // 2

    @pl.when(my_row < half)
    def _():
        chain()
        hop.start()

    forward(near, far)

    @pl.when((my_row >= half) & (my_row < n_rows - 1))
    def _():
        chain()
        hop.start()

    for copy in far:
        copy.wait_recv()

    def spread(index, _):
        c = index // n_rows
        r = index % n_rows
        marks = gathered[c, r, CAP * tile : (CAP + 1) * tile, :].astype(F32)
        tiles = [gathered[c, r, s * tile : (s + 1) * tile, :] for s in range(CAP)]
        where = [
            jnp.broadcast_to(marks[s : s + 1, :], (tile, blk)).astype(BF16) for s in range(CAP)
        ]
        base = (r * n_cols + c) * (tpd * tile)
        zero = jnp.zeros((tile, blk), BF16)
        for t in range(tpd):
            for j in range(per_row):
                total = zero
                for s in range(CAP):
                    total = total + jnp.where(where[s] == t * per_row + j, tiles[s], zero)
                dense[
                    pl.ds(pl.multiple_of(base + t * tile, tile), tile), j * blk : (j + 1) * blk
                ] = total
        return 0

    lax.fori_loop(0, n_rows * n_cols, spread, 0)

    ahead = lax.broadcasted_iota(jnp.int32, (tile, group), 1)
    down = lax.broadcasted_iota(jnp.int32, (tile, group), 0)
    for i in range(tpr):
        same = ahead == slot_ref[0, i] * tile + down
        order[i * tile : (i + 1) * tile, :] = jnp.where(same, 1.0, 0.0).astype(BF16)

    @pl.when(my_row == n_rows - 1)
    def _():
        chain()

    def product(r):
        rows = pl.ds(pl.multiple_of(r * group, group), group)
        return lax.dot_general(solved[...], dense[rows, :], NT, preferred_element_type=F32)

    parts = []
    for step in range(1, n_rows):
        partial[step] = product(lax.rem(my_row + step, n_rows)).astype(BF16)
        part = pltpu.make_async_remote_copy(
            src_ref=partial.at[step],
            dst_ref=arrived.at[step],
            send_sem=part_send.at[step],
            recv_sem=part_recv.at[step],
            device_id=row_peer(step),
            device_id_type=pl.DeviceIdType.MESH,
        )
        part.start()
        parts.append(part)
    total = product(my_row)
    for step in range(1, n_rows):
        parts[step - 1].wait_recv()
        total = total + arrived[step].astype(F32)
    mine = pl.ds(pl.multiple_of(my_col * cols, cols), cols)
    turned[mine, :] = total.astype(BF16)

    turn_near, turn_far = pair_up(
        turn_send,
        turn_recv,
        lambda index: turned.at[pl.ds(pl.multiple_of(index * cols, cols), cols)],
    )
    for copy in turn_far[:1] + turn_near:
        copy.start()
    forward(turn_near, turn_far)
    for copy in turn_far:
        copy.wait_recv()
    out[...] = lax.dot_general(
        order[...], turned[...], NT, preferred_element_type=F32
    ).astype(BF16)

    for copy in near + far + parts + turn_near + turn_far:
        copy.wait_send()

    @pl.when(my_row < n_rows - 1)
    def _():
        hop.wait_send()


def shards(
    n_rows,
    n_cols,
    rhs,
    couple_prev,
    diag_inverse,
    coupling,
    pair_block,
    pair_tile,
    pair_count,
    owner_slot,
    schur,
    surface_factor,
):
    cols, width = rhs.shape
    held, tile, blk = coupling.shape
    group = owner_slot.shape[1] * tile
    chunk = (CAP + 1) * tile
    dma = pltpu.SemaphoreType.DMA
    vmem = pl.BlockSpec(memory_space=pltpu.VMEM)
    hbm = pl.BlockSpec(memory_space=pltpu.HBM)
    scratch = [
        pltpu.VMEM((cols, width), F32),
        pltpu.VMEM((width, width), F32),
        pltpu.VMEM((width, width), F32),
        pltpu.VMEM((held, tile, blk), BF16),
        pltpu.SMEM((held,), jnp.int32),
        pltpu.SMEM((held,), jnp.int32),
        pltpu.SMEM((1,), jnp.int32),
        pltpu.SMEM(owner_slot.shape, jnp.int32),
        pltpu.VMEM((width, width), BF16),
        pltpu.VMEM((width, width), BF16),
        pltpu.VMEM((width, width), BF16),
        pltpu.VMEM((n_rows, chunk, blk), BF16),
        pltpu.VMEM((n_cols, n_rows, chunk, blk), BF16),
        pltpu.VMEM((n_rows * group, width), BF16),
        pltpu.VMEM((group, group), BF16),
        pltpu.VMEM((cols, width), BF16),
        pltpu.VMEM((cols, width), BF16),
        pltpu.VMEM((cols, width), F32),
        pltpu.VMEM((n_rows, cols, group), BF16),
        pltpu.VMEM((n_rows, cols, group), BF16),
        pltpu.VMEM((n_cols * cols, group), BF16),
        dma((8,)),
        dma((n_rows,)),
        dma((n_rows,)),
        dma((n_cols + 1,)),
        dma((n_cols + 1,)),
        dma((2,)),
        dma((n_rows,)),
        dma((n_rows,)),
        dma((n_cols + 1,)),
        dma((n_cols + 1,)),
    ]
    rows_w = pl.pallas_call(
        functools.partial(kernel, n_rows, n_cols),
        out_shape=jax.ShapeDtypeStruct((group, n_cols * cols), BF16),
        in_specs=[hbm] * 8,
        out_specs=vmem,
        scratch_shapes=scratch,
        compiler_params=pltpu.CompilerParams(
            collective_id=0,
            has_side_effects=True,
            vmem_limit_bytes=64 * 2**20 - 2**16,
        ),
        name="solve_and_route",
    )(rhs, couple_prev, diag_inverse, coupling, pair_block, pair_tile, pair_count, owner_slot)
    change = jnp.dot(rows_w, surface_factor, preferred_element_type=F32)
    return (schur.astype(F32) - change).astype(BF16)


def solution(mesh):
    placed = (
        P("col", "row"),
        P("row", None),
        P("row", None),
        P(("row", "col"), None, None),
        P(("row", "col")),
        P(("row", "col")),
        P(("row", "col")),
        P("row", None),
        P("row", "col"),
        P(None, "col"),
    )
    return jax.shard_map(
        functools.partial(shards, mesh.shape["row"], mesh.shape["col"]),
        mesh=mesh,
        in_specs=placed,
        out_specs=P("row", "col"),
        check_vma=False,
    )
```

profile of v0, /device:TPU:0, one launch (start us, length us, event | category | flops | bytes accessed | tf_op | source)
XLA Modules:
  0.0 44.2 jit_solution(18417477543681307102)
XLA Ops:
  0.7 36.8 %solve_and_route.1 = bf16[384,512]{1,0:T(8,128)(2,1)} custom-call(f32[64,1024]{1,0:T(8,128)} %rhs_hbm.1, f32[1024,1024]{1,0:T(8,128)} %couple_hbm.1, f32[1024,1024]{1,0:T(8,128)} %inverse_hbm.1, bf16[12,16,128]{2,1,0:T(8,128)(2,1)} %coupling_hbm.1, s32[12]{0:T(128)} %block_hbm.1, s32[12]{0:T(128)} %tile_hbm.1, s32[1]{0:T(128)S(6)} %copy.11.count_hbm, ...), custom_call_target="tpu_custom_call" | custom-call | tf_op jit(solution)/shard_map/solve_and_route/pallas_call | solution.py:376
  37.5 6.8 %subtract_convert_fusion = bf16[384,4096]{1,0:T(8,128)(2,1)} fusion(bf16[384,4096]{1,0:T(8,128)(2,1)} %param.18, bf16[384,512]{1,0:T(8,128)(2,1)} %solve_and_route.1, bf16[512,4096]{1,0:T(8,128)(2,1)} %param.19), kind=kOutput, calls=%fused_computation | convolution fusion | flops 1615331328 | bytes 10878976 | tf_op jit(solution)/shard_map/dot_general | solution.py:389
where the time goes:
time: 44.4 us; the launch traced here: 44.2 us
  Pallas kernels  36.8 us (83%)
  matrix products  6.75 us (15%)
  between operations  0.66 us (1%)
    pallas_call x1, Pallas kernels, shards(): pl.pallas_call(functools.partial(kernel, n_rows, n_cols), out_shape=jax.S...  36.8 us
    dot_general x1, matrix products, shards(): change = jnp.dot(rows_w, surface_factor, preferred_element_type=F32)  6.75 us

commit v1 on v0

--- a/solution.py
+++ b/solution.py
@@ -8,6 +8,8 @@
 from jax.sharding import PartitionSpec as P
 
 CAP = 3
+HOPS = 4
+VMEM = 64 * 2**20 - 2**16
 F32 = jnp.float32
 BF16 = jnp.bfloat16
 NT = (((1,), (1,)), ((), ()))
@@ -51,7 +53,6 @@
     order,
     solved,
     before,
-    right,
     partial,
     arrived,
     turned,
@@ -60,7 +61,8 @@
     swap_recv,
     share_send,
     share_recv,
-    hop_sem,
+    hop_send,
+    hop_recv,
     part_send,
     part_recv,
     turn_send,
@@ -189,6 +191,43 @@
     high, low = halves(inverse[...])
     inverse_hi[...] = high
     inverse_lo[...] = low
+    span = width // HOPS
+    hops = []
+    for h in range(HOPS):
+        ahead = slice(h * span, (h + 1) * span)
+        hops.append(
+            pltpu.make_async_remote_copy(
+                src_ref=solved.at[:, ahead],
+                dst_ref=before.at[:, ahead],
+                send_sem=hop_send.at[h],
+                recv_sem=hop_recv.at[h],
+                device_id=row_peer(1),
+                device_id_type=pl.DeviceIdType.MESH,
+            )
+        )
+
+    def chain(first, last):
+        value = rhs[...]
+        if not first:
+            for h in range(HOPS):
+                part = slice(h * span, (h + 1) * span)
+                hops[h].wait_recv()
+                value = value - dot(before[:, part], couple_hi[part, :])
+        high, low = halves(value)
+        stack = jnp.concatenate([high, low], axis=0)
+        for h in range(HOPS):
+            part = slice(h * span, (h + 1) * span)
+            both = dot(stack, inverse_hi[:, part])
+            solved[:, part] = (
+                both[:cols] + both[cols:] + dot(high, inverse_lo[:, part])
+            ).astype(BF16)
+            if not last:
+                hops[h].start()
+
+    @pl.when(my_row == 0)
+    def _():
+        chain(True, n_rows == 1)
+
     loads[6].wait()
     loads[7].wait()
 
@@ -202,41 +241,17 @@
     for copy in far[:1] + near:
         copy.start()
 
-    hop = pltpu.make_async_remote_copy(
-        src_ref=solved,
-        dst_ref=before,
-        send_sem=hop_sem.at[0],
-        recv_sem=hop_sem.at[1],
-        device_id=row_peer(1),
-        device_id_type=pl.DeviceIdType.MESH,
-    )
-
-    def chain():
-        right[...] = rhs[...]
-
-        @pl.when(my_row > 0)
-        def _():
-            hop.wait_recv()
-            known = before[...]
-            right[...] = rhs[...] - dot(known, couple_hi[...])
-
-        high, low = halves(right[...])
-        both = dot(jnp.concatenate([high, low], axis=0), inverse_hi[...])
-        solved[...] = (both[:cols] + both[cols:] + dot(high, inverse_lo[...])).astype(BF16)
-
     half = n_rows // 2
 
-    @pl.when(my_row < half)
-    def _():
-        chain()
-        hop.start()
+    @pl.when((my_row > 0) & (my_row < half))
+    def _():
+        chain(False, False)
 
     forward(near, far)
 
-    @pl.when((my_row >= half) & (my_row < n_rows - 1))
-    def _():
-        chain()
-        hop.start()
+    @pl.when((my_row > 0) & (my_row >= half) & (my_row < n_rows - 1))
+    def _():
+        chain(False, False)
 
     for copy in far:
         copy.wait_recv()
@@ -269,9 +284,9 @@
         same = ahead == slot_ref[0, i] * tile + down
         order[i * tile : (i + 1) * tile, :] = jnp.where(same, 1.0, 0.0).astype(BF16)
 
-    @pl.when(my_row == n_rows - 1)
-    def _():
-        chain()
+    @pl.when((my_row > 0) & (my_row == n_rows - 1))
+    def _():
+        chain(False, True)
 
     def product(r):
         rows = pl.ds(pl.multiple_of(r * group, group), group)
@@ -316,7 +331,12 @@
 
     @pl.when(my_row < n_rows - 1)
     def _():
-        hop.wait_send()
+        for hop in hops:
+            hop.wait_send()
+
+
+def update(rows_w, factor, schur, out):
+    out[...] = (schur[...].astype(F32) - dot(rows_w[...], factor[...])).astype(BF16)
 
 
 def shards(
@@ -358,7 +378,6 @@
         pltpu.VMEM((group, group), BF16),
         pltpu.VMEM((cols, width), BF16),
         pltpu.VMEM((cols, width), BF16),
-        pltpu.VMEM((cols, width), F32),
         pltpu.VMEM((n_rows, cols, group), BF16),
         pltpu.VMEM((n_rows, cols, group), BF16),
         pltpu.VMEM((n_cols * cols, group), BF16),
@@ -367,7 +386,8 @@
         dma((n_rows,)),
         dma((n_cols + 1,)),
         dma((n_cols + 1,)),
-        dma((2,)),
+        dma((HOPS,)),
+        dma((HOPS,)),
         dma((n_rows,)),
         dma((n_rows,)),
         dma((n_cols + 1,)),
@@ -382,12 +402,26 @@
         compiler_params=pltpu.CompilerParams(
             collective_id=0,
             has_side_effects=True,
-            vmem_limit_bytes=64 * 2**20 - 2**16,
+            vmem_limit_bytes=VMEM,
         ),
         name="solve_and_route",
     )(rhs, couple_prev, diag_inverse, coupling, pair_block, pair_tile, pair_count, owner_slot)
-    change = jnp.dot(rows_w, surface_factor, preferred_element_type=F32)
-    return (schur.astype(F32) - change).astype(BF16)
+    rows, columns = schur.shape
+    depth = surface_factor.shape[0]
+    step = 4 * blk if columns % (4 * blk) == 0 else blk
+    return pl.pallas_call(
+        update,
+        out_shape=jax.ShapeDtypeStruct((rows, columns), BF16),
+        grid=(columns // step,),
+        in_specs=[
+            pl.BlockSpec((rows, depth), lambda i: (0, 0)),
+            pl.BlockSpec((depth, step), lambda i: (0, i)),
+            pl.BlockSpec((rows, step), lambda i: (0, i)),
+        ],
+        out_specs=pl.BlockSpec((rows, step), lambda i: (0, i)),
+        compiler_params=pltpu.CompilerParams(vmem_limit_bytes=VMEM),
+        name="slab_update",
+    )(rows_w, surface_factor, schur)
 
 
 def solution(mesh):

time: 44.4 us -> 46.3 us (1.043)
  Pallas kernels: 36.8 us -> 45.3 us
  matrix products: 6.75 us -> 0 us
    pallas_call x0 -> x1, Pallas kernels: none -> 8.42 us  [shards(): pl.pallas_call(update, out_shape=jax.ShapeDtypeStruct((rows, columns), BF...]
    dot_general x1 -> x0, matrix products: 6.75 us -> none  [shards(): change = jnp.dot(rows_w, surface_factor, preferred_element_type=F32)]
where the time goes in v1:
time: 46.3 us; the launch traced here: 46 us
  Pallas kernels  45.3 us (98%)
  between operations  0.66 us (1%)
    pallas_call x1, Pallas kernels, shards(): pl.pallas_call(functools.partial(kernel, n_rows, n_cols), out_shape=jax.S...  36.9 us
    pallas_call x1, Pallas kernels, shards(): pl.pallas_call(update, out_shape=jax.ShapeDtypeStruct((rows, columns), BF...  8.42 us

profile of v1, /device:TPU:0, one launch (start us, length us, event | category | flops | bytes accessed | tf_op | source)
XLA Modules:
  0.0 46.0 jit_solution(13585913827660246187)
XLA Ops:
  0.7 36.9 %solve_and_route.1.rows_w = bf16[384,512]{1,0:T(8,128)(2,1)} custom-call(f32[64,1024]{1,0:T(8,128)} %rhs_hbm.1, f32[1024,1024]{1,0:T(8,128)} %couple_hbm.1, f32[1024,1024]{1,0:T(8,128)} %inverse_hbm.1, bf16[12,16,128]{2,1,0:T(8,128)(2,1)} %coupling_hbm.1, s32[12]{0:T(128)} %block_hbm.1, s32[12]{0:T(128)} %tile_hbm.1, s32[1]{0:T(128)S(6)} %copy.11.count_hbm, ...), custom_call_target="tpu_custom_call" | custom-call | tf_op jit(solution)/shard_map/solve_and_route/pallas_call | solution.py:396
  37.5 8.4 %slab_update.1 = bf16[384,4096]{1,0:T(8,128)(2,1)} custom-call(bf16[384,512]{1,0:T(8,128)(2,1)} %solve_and_route.1.rows_w, bf16[512,4096]{1,0:T(8,128)(2,1)} %factor.1, bf16[384,4096]{1,0:T(8,128)(2,1)} %schur.1), custom_call_target="tpu_custom_call" | custom-call | tf_op jit(solution)/shard_map/slab_update/pallas_call | solution.py:412

commit v2 on v1

--- a/solution.py
+++ b/solution.py
@@ -9,7 +9,7 @@
 
 CAP = 3
 HOPS = 4
-VMEM = 64 * 2**20 - 2**16
+VMEM = 64 * 2**20
 F32 = jnp.float32
 BF16 = jnp.bfloat16
 NT = (((1,), (1,)), ((), ()))
@@ -186,11 +186,6 @@
         swap.start()
         swaps.append(swap)
 
-    loads[4].wait()
-    loads[5].wait()
-    high, low = halves(inverse[...])
-    inverse_hi[...] = high
-    inverse_lo[...] = low
     span = width // HOPS
     hops = []
     for h in range(HOPS):
@@ -224,16 +219,18 @@
             if not last:
                 hops[h].start()
 
+    def split():
+        high, low = halves(inverse[...])
+        inverse_hi[...] = high
+        inverse_lo[...] = low
+
+    loads[4].wait()
+    loads[5].wait()
+
     @pl.when(my_row == 0)
     def _():
+        split()
         chain(True, n_rows == 1)
-
-    loads[6].wait()
-    loads[7].wait()
-
-    @pl.when(my_row > 0)
-    def _():
-        couple_hi[...] = couple[...].astype(BF16)
 
     for swap in swaps:
         swap.wait()
@@ -241,6 +238,14 @@
     for copy in far[:1] + near:
         copy.start()
 
+    loads[6].wait()
+    loads[7].wait()
+
+    @pl.when(my_row > 0)
+    def _():
+        split()
+        couple_hi[...] = couple[...].astype(BF16)
+
     half = n_rows // 2
 
     @pl.when((my_row > 0) & (my_row < half))
@@ -261,16 +266,28 @@
         r = index % n_rows
         marks = gathered[c, r, CAP * tile : (CAP + 1) * tile, :].astype(F32)
         tiles = [gathered[c, r, s * tile : (s + 1) * tile, :] for s in range(CAP)]
-        where = [
-            jnp.broadcast_to(marks[s : s + 1, :], (tile, blk)).astype(BF16) for s in range(CAP)
-        ]
+        rows = [jnp.broadcast_to(marks[s : s + 1, :], (tile, blk)) for s in range(CAP)]
         base = (r * n_cols + c) * (tpd * tile)
-        zero = jnp.zeros((tile, blk), BF16)
+
+        def gate(test):
+            return jnp.where(test, 1.0, 0.0).astype(BF16)
+
+        gates = []
+        kept = []
+        for s in range(CAP):
+            least = [rows[s] >= float(t * per_row) for t in range(tpd + 1)]
+            kept.append(
+                [tiles[s] * gate(least[t] & ~least[t + 1]) for t in range(tpd)]
+            )
+            local = rows[s]
+            for t in range(1, tpd):
+                local = local - jnp.where(least[t], float(per_row), 0.0)
+            gates.append([gate(local == float(j)) for j in range(per_row)])
         for t in range(tpd):
             for j in range(per_row):
-                total = zero
-                for s in range(CAP):
-                    total = total + jnp.where(where[s] == t * per_row + j, tiles[s], zero)
+                total = kept[0][t] * gates[0][j]
+                for s in range(1, CAP):
+                    total = total + kept[s][t] * gates[s][j]
                 dense[
                     pl.ds(pl.multiple_of(base + t * tile, tile), tile), j * blk : (j + 1) * blk
                 ] = total
@@ -290,7 +307,7 @@
 
     def product(r):
         rows = pl.ds(pl.multiple_of(r * group, group), group)
-        return lax.dot_general(solved[...], dense[rows, :], NT, preferred_element_type=F32)
+        return lax.dot_general(dense[rows, :], solved[...], NT, preferred_element_type=F32).T
 
     parts = []
     for step in range(1, n_rows):
@@ -333,10 +350,6 @@
     def _():
         for hop in hops:
             hop.wait_send()
-
-
-def update(rows_w, factor, schur, out):
-    out[...] = (schur[...].astype(F32) - dot(rows_w[...], factor[...])).astype(BF16)
 
 
 def shards(
@@ -393,6 +406,7 @@
         dma((n_cols + 1,)),
         dma((n_cols + 1,)),
     ]
+    beside = 2 * (schur.size + surface_factor.size)
     rows_w = pl.pallas_call(
         functools.partial(kernel, n_rows, n_cols),
         out_shape=jax.ShapeDtypeStruct((group, n_cols * cols), BF16),
@@ -402,26 +416,12 @@
         compiler_params=pltpu.CompilerParams(
             collective_id=0,
             has_side_effects=True,
-            vmem_limit_bytes=VMEM,
+            vmem_limit_bytes=VMEM - beside - 2**20,
         ),
         name="solve_and_route",
     )(rhs, couple_prev, diag_inverse, coupling, pair_block, pair_tile, pair_count, owner_slot)
-    rows, columns = schur.shape
-    depth = surface_factor.shape[0]
-    step = 4 * blk if columns % (4 * blk) == 0 else blk
-    return pl.pallas_call(
-        update,
-        out_shape=jax.ShapeDtypeStruct((rows, columns), BF16),
-        grid=(columns // step,),
-        in_specs=[
-            pl.BlockSpec((rows, depth), lambda i: (0, 0)),
-            pl.BlockSpec((depth, step), lambda i: (0, i)),
-            pl.BlockSpec((rows, step), lambda i: (0, i)),
-        ],
-        out_specs=pl.BlockSpec((rows, step), lambda i: (0, i)),
-        compiler_params=pltpu.CompilerParams(vmem_limit_bytes=VMEM),
-        name="slab_update",
-    )(rows_w, surface_factor, schur)
+    change = jnp.dot(rows_w, surface_factor, preferred_element_type=F32)
+    return (schur.astype(F32) - change).astype(BF16)
 
 
 def solution(mesh):

time: 46.3 us -> 43.1 us (0.931)
  Pallas kernels: 45.3 us -> 37.8 us
  matrix products: 0 us -> 4.46 us
    pallas_call x1 -> x0, Pallas kernels: 8.42 us -> none  [shards(): pl.pallas_call(update, out_shape=jax.ShapeDtypeStruct((rows, columns), BF...]
    dot_general x0 -> x1, matrix products: none -> 4.46 us  [shards(): change = jnp.dot(rows_w, surface_factor, preferred_element_type=F32)]
    pallas_call x1, Pallas kernels: 36.9 us -> 37.8 us  [shards(): pl.pallas_call(functools.partial(kernel, n_rows, n_cols), out_shape=jax.S...]
where the time goes in v2:
time: 43.1 us; the launch traced here: 43 us
  Pallas kernels  37.8 us (88%)
  matrix products  4.46 us (10%)
  between operations  0.69 us (2%)
    pallas_call x1, Pallas kernels, shards(): pl.pallas_call(functools.partial(kernel, n_rows, n_cols), out_shape=jax.S...  37.8 us
    dot_general x1, matrix products, shards(): change = jnp.dot(rows_w, surface_factor, preferred_element_type=F32)  4.46 us

profile of v2, /device:TPU:0, one launch (start us, length us, event | category | flops | bytes accessed | tf_op | source)
XLA Modules:
  0.0 43.0 jit_solution(13015924775654235470)
XLA Ops:
  0.7 0.0 copy-start
  0.7 0.0 copy-start.1
  0.7 37.8 %solve_and_route.1 = bf16[384,512]{1,0:T(8,128)(2,1)} custom-call(f32[64,1024]{1,0:T(8,128)} %rhs_hbm.1, f32[1024,1024]{1,0:T(8,128)} %couple_hbm.1, f32[1024,1024]{1,0:T(8,128)} %inverse_hbm.1, bf16[12,16,128]{2,1,0:T(8,128)(2,1)} %coupling_hbm.1, s32[12]{0:T(128)} %block_hbm.1, s32[12]{0:T(128)} %tile_hbm.1, s32[1]{0:T(128)S(6)} %copy.11.count_hbm, ...), custom_call_target="tpu_custom_call" | custom-call | tf_op jit(solution)/shard_map/solve_and_route/pallas_call | solution.py:410
  38.5 0.0 copy-done
  38.5 0.0 copy-done.1
  38.5 4.5 %subtract_convert_fusion = bf16[384,4096]{1,0:T(8,128)(2,1)} fusion(bf16[384,4096]{1,0:T(8,128)(2,1)S(1)} %copy-done.1, bf16[384,512]{1,0:T(8,128)(2,1)} %solve_and_route.1, bf16[512,4096]{1,0:T(8,128)(2,1)S(1)} %copy-done), kind=kOutput, calls=%fused_computation | convolution fusion | flops 1615331328 | bytes 10878976 | tf_op jit(solution)/shard_map/dot_general | solution.py:423
Async XLA Ops:
  0.7 37.8 %copy-start = (bf16[512,4096]{1,0:T(8,128)(2,1)S(1)}, bf16[512,4096]{1,0:T(8,128)(2,1)}, u32[]{:S(2)}) copy-start(bf16[512,4096]{1,0:T(8,128)(2,1)} %param.19) | copy-start | bytes 12582916
  0.7 37.8 %copy-start.1 = (bf16[384,4096]{1,0:T(8,128)(2,1)S(1)}, bf16[384,4096]{1,0:T(8,128)(2,1)}, u32[]{:S(2)}) copy-start(bf16[384,4096]{1,0:T(8,128)(2,1)} %param.18) | copy-start | bytes 9437188

commit v3 on v2

--- a/solution.py
+++ b/solution.py
@@ -103,7 +103,7 @@
     pair = 2 if n_cols % 2 == 0 else 1
     line = n_cols // pair
 
-    def pair_up(send, recv, block):
+    def pair_up(send, recv, block, base=0):
         lane = lax.rem(my_col, pair)
         major = my_col // pair
         near, far = [], []
@@ -112,8 +112,8 @@
             return pltpu.make_async_remote_copy(
                 src_ref=block(index),
                 dst_ref=block(index),
-                send_sem=send.at[number],
-                recv_sem=recv.at[number],
+                send_sem=send.at[base + number],
+                recv_sem=recv.at[base + number],
                 device_id={"col": target},
                 device_id_type=pl.DeviceIdType.MESH,
             )
@@ -305,45 +305,61 @@
     def _():
         chain(False, True)
 
-    def product(r):
-        rows = pl.ds(pl.multiple_of(r * group, group), group)
+    shares, _, wide = turned.shape
+
+    def product(r, p):
+        rows = pl.ds(pl.multiple_of(r * group + p * wide, wide), wide)
         return lax.dot_general(dense[rows, :], solved[...], NT, preferred_element_type=F32).T
 
     parts = []
-    for step in range(1, n_rows):
-        partial[step] = product(lax.rem(my_row + step, n_rows)).astype(BF16)
-        part = pltpu.make_async_remote_copy(
-            src_ref=partial.at[step],
-            dst_ref=arrived.at[step],
-            send_sem=part_send.at[step],
-            recv_sem=part_recv.at[step],
-            device_id=row_peer(step),
-            device_id_type=pl.DeviceIdType.MESH,
-        )
-        part.start()
-        parts.append(part)
-    total = product(my_row)
-    for step in range(1, n_rows):
-        parts[step - 1].wait_recv()
-        total = total + arrived[step].astype(F32)
-    mine = pl.ds(pl.multiple_of(my_col * cols, cols), cols)
-    turned[mine, :] = total.astype(BF16)
-
-    turn_near, turn_far = pair_up(
-        turn_send,
-        turn_recv,
-        lambda index: turned.at[pl.ds(pl.multiple_of(index * cols, cols), cols)],
-    )
-    for copy in turn_far[:1] + turn_near:
-        copy.start()
-    forward(turn_near, turn_far)
-    for copy in turn_far:
-        copy.wait_recv()
-    out[...] = lax.dot_general(
-        order[...], turned[...], NT, preferred_element_type=F32
-    ).astype(BF16)
-
-    for copy in near + far + parts + turn_near + turn_far:
+    for p in range(shares):
+        for step in range(1, n_rows):
+            partial[step, p] = product(lax.rem(my_row + step, n_rows), p).astype(BF16)
+            part = pltpu.make_async_remote_copy(
+                src_ref=partial.at[step, p],
+                dst_ref=arrived.at[step, p],
+                send_sem=part_send.at[p * n_rows + step],
+                recv_sem=part_recv.at[p * n_rows + step],
+                device_id=row_peer(step),
+                device_id_type=pl.DeviceIdType.MESH,
+            )
+            part.start()
+            parts.append(part)
+
+    def slab(index):
+        return pl.ds(pl.multiple_of(index * cols, cols), cols)
+
+    turns = []
+    for p in range(shares):
+        total = product(my_row, p)
+        for step in range(1, n_rows):
+            parts[p * (n_rows - 1) + step - 1].wait_recv()
+            total = total + arrived[step, p].astype(F32)
+        turned[p, slab(my_col), :] = total.astype(BF16)
+        turn = pair_up(
+            turn_send,
+            turn_recv,
+            lambda index, p=p: turned.at[p, slab(index)],
+            p * (n_cols + 1),
+        )
+        for copy in turn[1][:1] + turn[0]:
+            copy.start()
+        turns.append(turn)
+    for turn in turns:
+        forward(*turn)
+    total = None
+    for p, turn in enumerate(turns):
+        for copy in turn[1]:
+            copy.wait_recv()
+        moved = lax.dot_general(
+            order[:, p * wide : (p + 1) * wide], turned[p], NT, preferred_element_type=F32
+        )
+        total = moved if total is None else total + moved
+    out[...] = total.astype(BF16)
+
+    for turn in turns:
+        parts = parts + turn[0] + turn[1]
+    for copy in near + far + parts:
         copy.wait_send()
 
     @pl.when(my_row < n_rows - 1)
@@ -370,6 +386,7 @@
     held, tile, blk = coupling.shape
     group = owner_slot.shape[1] * tile
     chunk = (CAP + 1) * tile
+    shares = 3 if group % (3 * blk) == 0 else 1
     dma = pltpu.SemaphoreType.DMA
     vmem = pl.BlockSpec(memory_space=pltpu.VMEM)
     hbm = pl.BlockSpec(memory_space=pltpu.HBM)
@@ -391,9 +408,9 @@
         pltpu.VMEM((group, group), BF16),
         pltpu.VMEM((cols, width), BF16),
         pltpu.VMEM((cols, width), BF16),
-        pltpu.VMEM((n_rows, cols, group), BF16),
-        pltpu.VMEM((n_rows, cols, group), BF16),
-        pltpu.VMEM((n_cols * cols, group), BF16),
+        pltpu.VMEM((n_rows, shares, cols, group // shares), BF16),
+        pltpu.VMEM((n_rows, shares, cols, group // shares), BF16),
+        pltpu.VMEM((shares, n_cols * cols, group // shares), BF16),
         dma((8,)),
         dma((n_rows,)),
         dma((n_rows,)),
@@ -401,10 +418,10 @@
         dma((n_cols + 1,)),
         dma((HOPS,)),
         dma((HOPS,)),
-        dma((n_rows,)),
-        dma((n_rows,)),
-        dma((n_cols + 1,)),
-        dma((n_cols + 1,)),
+        dma((n_rows * shares,)),
+        dma((n_rows * shares,)),
+        dma(((n_cols + 1) * shares,)),
+        dma(((n_cols + 1) * shares,)),
     ]
     beside = 2 * (schur.size + surface_factor.size)
     rows_w = pl.pallas_call(

time: 43.1 us -> 42.6 us (0.988)
  Pallas kernels: 37.8 us -> 37.3 us
    pallas_call x1, Pallas kernels: 37.8 us -> 37.3 us  [shards(): pl.pallas_call(functools.partial(kernel, n_rows, n_cols), out_shape=jax.S...]
where the time goes in v3:
time: 42.6 us; the launch traced here: 42.4 us
  Pallas kernels  37.3 us (88%)
  matrix products  4.46 us (10%)
  between operations  0.69 us (2%)
    pallas_call x1, Pallas kernels, shards(): pl.pallas_call(functools.partial(kernel, n_rows, n_cols), out_shape=jax.S...  37.3 us
    dot_general x1, matrix products, shards(): change = jnp.dot(rows_w, surface_factor, preferred_element_type=F32)  4.46 us

profile of v3, /device:TPU:0, one launch (start us, length us, event | category | flops | bytes accessed | tf_op | source)
XLA Modules:
  0.0 42.4 jit_solution(14038386782841146127)
XLA Ops:
  0.7 0.0 copy-start
  0.7 0.0 copy-start.1
  0.7 37.3 %solve_and_route.1 = bf16[384,512]{1,0:T(8,128)(2,1)} custom-call(f32[64,1024]{1,0:T(8,128)} %rhs_hbm.1, f32[1024,1024]{1,0:T(8,128)} %couple_hbm.1, f32[1024,1024]{1,0:T(8,128)} %inverse_hbm.1, bf16[12,16,128]{2,1,0:T(8,128)(2,1)} %coupling_hbm.1, s32[12]{0:T(128)} %block_hbm.1, s32[12]{0:T(128)} %tile_hbm.1, s32[1]{0:T(128)S(6)} %copy.11.count_hbm, ...), custom_call_target="tpu_custom_call" | custom-call | tf_op jit(solution)/shard_map/solve_and_route/pallas_call | solution.py:427
  38.0 0.0 copy-done
  38.0 0.0 copy-done.1
  38.0 4.5 %subtract_convert_fusion = bf16[384,4096]{1,0:T(8,128)(2,1)} fusion(bf16[384,4096]{1,0:T(8,128)(2,1)S(1)} %copy-done.1, bf16[384,512]{1,0:T(8,128)(2,1)} %solve_and_route.1, bf16[512,4096]{1,0:T(8,128)(2,1)S(1)} %copy-done), kind=kOutput, calls=%fused_computation | convolution fusion | flops 1615331328 | bytes 10878976 | tf_op jit(solution)/shard_map/dot_general | solution.py:440
Async XLA Ops:
  0.7 37.3 %copy-start = (bf16[512,4096]{1,0:T(8,128)(2,1)S(1)}, bf16[512,4096]{1,0:T(8,128)(2,1)}, u32[]{:S(2)}) copy-start(bf16[512,4096]{1,0:T(8,128)(2,1)} %param.19) | copy-start | bytes 12582916
  0.7 37.3 %copy-start.1 = (bf16[384,4096]{1,0:T(8,128)(2,1)S(1)}, bf16[384,4096]{1,0:T(8,128)(2,1)}, u32[]{:S(2)}) copy-start(bf16[384,4096]{1,0:T(8,128)(2,1)} %param.18) | copy-start | bytes 9437188

commit v4 on v3

--- a/solution.py
+++ b/solution.py
@@ -9,6 +9,7 @@
 
 CAP = 3
 HOPS = 4
+LOTS = 4
 VMEM = 64 * 2**20
 F32 = jnp.float32
 BF16 = jnp.bfloat16
@@ -82,11 +83,12 @@
         (tile_hbm, tile_ref),
         (count_hbm, count_ref),
         (coupling_hbm, coupling),
-        (inverse_hbm, inverse),
         (rhs_hbm, rhs),
-        (couple_hbm, couple),
         (slot_hbm, slot_ref),
     ]
+    lots = [slice(i * (width // LOTS), (i + 1) * (width // LOTS)) for i in range(LOTS)]
+    pairs += [(inverse_hbm.at[lot], inverse.at[lot]) for lot in lots]
+    pairs += [(couple_hbm.at[lot], couple.at[lot]) for lot in lots]
     loads = [
         pltpu.make_async_copy(source, target, load_sem.at[i])
         for i, (source, target) in enumerate(pairs)
@@ -220,9 +222,11 @@
                 hops[h].start()
 
     def split():
-        high, low = halves(inverse[...])
-        inverse_hi[...] = high
-        inverse_lo[...] = low
+        for i, lot in enumerate(lots):
+            loads[6 + i].wait()
+            high, low = halves(inverse[lot, :])
+            inverse_hi[lot, :] = high
+            inverse_lo[lot, :] = low
 
     loads[4].wait()
     loads[5].wait()
@@ -238,13 +242,12 @@
     for copy in far[:1] + near:
         copy.start()
 
-    loads[6].wait()
-    loads[7].wait()
-
     @pl.when(my_row > 0)
     def _():
         split()
-        couple_hi[...] = couple[...].astype(BF16)
+        for i, lot in enumerate(lots):
+            loads[6 + LOTS + i].wait()
+            couple_hi[lot, :] = couple[lot, :].astype(BF16)
 
     half = n_rows // 2
 
@@ -292,6 +295,11 @@
                     pl.ds(pl.multiple_of(base + t * tile, tile), tile), j * blk : (j + 1) * blk
                 ] = total
         return 0
+
+    @pl.when(my_row == 0)
+    def _():
+        for load in loads[6 + LOTS :]:
+            load.wait()
 
     lax.fori_loop(0, n_rows * n_cols, spread, 0)
 
@@ -411,7 +419,7 @@
         pltpu.VMEM((n_rows, shares, cols, group // shares), BF16),
         pltpu.VMEM((n_rows, shares, cols, group // shares), BF16),
         pltpu.VMEM((shares, n_cols * cols, group // shares), BF16),
-        dma((8,)),
+        dma((6 + 2 * LOTS,)),
         dma((n_rows,)),
         dma((n_rows,)),
         dma((n_cols + 1,)),

time: 42.6 us -> 42.6 us (level)
  no operation moved by 1% of the time
where the time goes in v4:
time: 42.6 us; the launch traced here: 42.5 us
  Pallas kernels  37.3 us (88%)
  matrix products  4.46 us (10%)
  between operations  0.69 us (2%)
    pallas_call x1, Pallas kernels, shards(): pl.pallas_call(functools.partial(kernel, n_rows, n_cols), out_shape=jax.S...  37.3 us
    dot_general x1, matrix products, shards(): change = jnp.dot(rows_w, surface_factor, preferred_element_type=F32)  4.46 us

profile of v4, /device:TPU:0, one launch (start us, length us, event | category | flops | bytes accessed | tf_op | source)
XLA Modules:
  0.0 42.5 jit_solution(697758630064524075)
XLA Ops:
  0.7 0.0 copy-start
  0.7 0.0 copy-start.1
  0.7 37.3 %solve_and_route.1 = bf16[384,512]{1,0:T(8,128)(2,1)} custom-call(f32[64,1024]{1,0:T(8,128)} %rhs_hbm.1, f32[1024,1024]{1,0:T(8,128)} %couple_hbm.1, f32[1024,1024]{1,0:T(8,128)} %inverse_hbm.1, bf16[12,16,128]{2,1,0:T(8,128)(2,1)} %coupling_hbm.1, s32[12]{0:T(128)} %block_hbm.1, s32[12]{0:T(128)} %tile_hbm.1, s32[1]{0:T(128)S(6)} %copy.11.count_hbm, ...), custom_call_target="tpu_custom_call" | custom-call | tf_op jit(solution)/shard_map/solve_and_route/pallas_call | solution.py:435
  38.0 0.0 copy-done
  38.0 0.0 copy-done.1
  38.0 4.5 %subtract_convert_fusion = bf16[384,4096]{1,0:T(8,128)(2,1)} fusion(bf16[384,4096]{1,0:T(8,128)(2,1)S(1)} %copy-done.1, bf16[384,512]{1,0:T(8,128)(2,1)} %solve_and_route.1, bf16[512,4096]{1,0:T(8,128)(2,1)S(1)} %copy-done), kind=kOutput, calls=%fused_computation | convolution fusion | flops 1615331328 | bytes 10878976 | tf_op jit(solution)/shard_map/dot_general | solution.py:448
Async XLA Ops:
  0.7 37.3 %copy-start = (bf16[512,4096]{1,0:T(8,128)(2,1)S(1)}, bf16[512,4096]{1,0:T(8,128)(2,1)}, u32[]{:S(2)}) copy-start(bf16[512,4096]{1,0:T(8,128)(2,1)} %param.19) | copy-start | bytes 12582916
  0.7 37.3 %copy-start.1 = (bf16[384,4096]{1,0:T(8,128)(2,1)S(1)}, bf16[384,4096]{1,0:T(8,128)(2,1)}, u32[]{:S(2)}) copy-start(bf16[384,4096]{1,0:T(8,128)(2,1)} %param.18) | copy-start | bytes 9437188
